TPU v7x, 1024 devices: a whole 8x8x8 slice. The times are simulated.
1024 devices in a mesh: fsdp: 64 (over x, y_lo, core), dp: 16 (over y_hi, z).
Axes of the slice: x: 8, y: 8 (y_hi: 2, y_lo: 4; y = y_hi * 4 + y_lo), z: 8, core: 2. Of those that a mesh axis runs over, the one named last changes fastest.
Arguments:
- activations: bfloat16 [16, 16384, 4096], P('dp', 'fsdp'), may hold values from -16 to 16
- cotangents: bfloat16 [16, 16384, 512], P('dp', 'fsdp'), may hold values from -0.046875 to 0.046875
- momentum: float32 [16, 4096, 512], P('dp', 'fsdp'), may hold values from -6 to 6
- freq_index: int32 [256], replicated, may hold values from 0 to 4095, as said below
Outputs:
- new_momentum: float32 [16, 4096, 512], P('dp', 'fsdp')
- update: float32 [4096, 512], P('fsdp')
Inputs may be any that keep to these rules, and one draw needn't show every extreme that they name: `freq_index`: 256 distinct indices in any order; 0 and 4095 are always among them.
All inputs are finite; a program needn't handle non-finite values.
Results may differ from a plain program's by a relative error of at most 0.0003.
Values sent between devices are 32-bit elements; how exact they have to be, the bound alone decides.
A program may use at most 128 MiB of HBM per device.

v0:
```python
import jax
import jax.numpy as jnp
from jax import lax
from jax.sharding import PartitionSpec as P

BLOCK = 64


momentum_decay = 0.999


def cosine_basis(side):
    wave = jnp.arange(side, dtype=jnp.float32)[:, None]
    sample = jnp.arange(side, dtype=jnp.float32)[None, :]
    factor = jnp.where(
        wave == 0.0, jnp.sqrt(jnp.float32(1.0) / side), jnp.sqrt(jnp.float32(2.0) / side)
    )
    return factor * jnp.cos(jnp.pi * (2.0 * sample + 1.0) * wave / (2.0 * side))


def forward(matrix, basis_mat):
    row_count, col_count = matrix.shape
    blocks = matrix.reshape(row_count // BLOCK, BLOCK, col_count // BLOCK, BLOCK)
    result = jnp.einsum(
        "ka,iajb,lb->ikjl", basis_mat, blocks, basis_mat, precision=lax.Precision.HIGHEST
    )
    return result.reshape(row_count, col_count)


def inverse(matrix, basis_mat):
    row_count, col_count = matrix.shape
    blocks = matrix.reshape(row_count // BLOCK, BLOCK, col_count // BLOCK, BLOCK)
    result = jnp.einsum(
        "ka,ikjl,lb->iajb", basis_mat, blocks, basis_mat, precision=lax.Precision.HIGHEST
    )
    return result.reshape(row_count, col_count)


def select_coeffs(coeffs, freq_index):
    row_count, col_count = coeffs.shape
    blocks = coeffs.reshape(row_count // BLOCK, BLOCK, col_count // BLOCK, BLOCK)
    wave_row = freq_index // BLOCK
    wave_col = freq_index % BLOCK
    return jnp.moveaxis(blocks[:, wave_row, :, wave_col], 0, -1)


def drop_selected(coeffs, freq_index):
    row_count, col_count = coeffs.shape
    flat_ids = jnp.arange(BLOCK * BLOCK, dtype=jnp.int32)
    taken = jnp.any(flat_ids[None, :] == freq_index[:, None], axis=0)
    keeper = 1.0 - taken.reshape(BLOCK, BLOCK).astype(jnp.float32)
    blocks = coeffs.reshape(row_count // BLOCK, BLOCK, col_count // BLOCK, BLOCK)
    return (blocks * keeper[None, :, None, :]).reshape(row_count, col_count)


def scatter_back(values, freq_index, row_count, col_count):
    wave_row = freq_index // BLOCK
    wave_col = freq_index % BLOCK
    blocks = jnp.zeros((row_count // BLOCK, BLOCK, col_count // BLOCK, BLOCK), jnp.float32)
    blocks = blocks.at[:, wave_row, :, wave_col].set(jnp.moveaxis(values, -1, 0))
    return blocks.reshape(row_count, col_count)


def shards(activations, cotangents, momentum, freq_index):
    basis_mat = cosine_basis(BLOCK)
    tokens_in = activations[0]
    grads_in = cotangents[0]
    held_state = momentum[0]
    row_count = held_state.shape[0]
    col_count = held_state.shape[1]
    incoming = lax.psum_scatter(
        lax.dot_general(
            tokens_in, grads_in, (((0,), (0,)), ((), ())), preferred_element_type=jnp.float32
        ),
        "fsdp",
        scatter_dimension=0,
        tiled=True,
    )
    coeffs = forward(momentum_decay * held_state + incoming, basis_mat)
    picked = select_coeffs(coeffs, freq_index)
    new_state = inverse(drop_selected(coeffs, freq_index), basis_mat)
    group_count = lax.axis_size("dp")
    everyone = lax.all_gather(picked[None], "dp", axis=0, tiled=True)
    summed = jnp.sum(everyone, axis=0)
    update = inverse(
        scatter_back(summed / group_count, freq_index, row_count, col_count), basis_mat
    )
    return (new_state[None], update)


def solution(mesh):
    return jax.shard_map(
        shards,
        mesh=mesh,
        in_specs=(P("dp", "fsdp", None), P("dp", "fsdp", None), P("dp", "fsdp", None), P()),
        out_specs=(P("dp", "fsdp", None), P("fsdp", None)),
        check_vma=False,
    )
```

profile of v0, /device:TPU:1, one launch (start us, length us, event | category | flops | bytes accessed | tf_op | source)
XLA Modules:
  0.0 417.9 jit_solution(11053068342132441255)
XLA Ops:
  7.2 0.0 copy-start
  7.2 0.0 reduce-scatter.2.cloned.1.call-start
  7.2 1.5 copy-done
  8.8 5.5 %fusion.1 = f32[4096,512]{1,0:T(8,128)} fusion(bf16[1,256,4096]{2,1,0:T(8,128)(2,1)S(1)} %copy-done, bf16[1,256,512]{2,1,0:T(8,128)(2,1)} %param.5), kind=kOutput, calls=%fused_computation.4 | convolution fusion | flops 1073741824 | bytes 10747904 | tf_op jit(solution)/shard_map/dot_general | solution.py:72
  14.2 0.0 copy-start.2
  14.2 0.0 copy-start.1
  14.2 0.0 reduce-scatter.2.cloned.1.call-update
  14.2 0.7 copy-done.2
  14.9 0.6 fusion
  15.5 0.1 sub.23
  15.7 306.4 %reduce-scatter.2.cloned.1.call-done = f32[64,512]{1,0:T(8,128)} async-done(((f32[4096,512]{1,0:T(8,128)}), f32[64,512]{1,0:T(8,128)}) %reduce-scatter.2.cloned.1.call-update) | async-done | bytes 131088 | tf_op jit(solution)/shard_map/reduce_scatter | solution.py:71
  322.1 0.0 copy-done.1
  322.1 0.9 bitcast_add_fusion
  323.0 0.1 copy.46
  323.1 1.0 fusion.15
  324.1 0.5 fusion.13
  324.6 0.5 fusion.4
  325.2 0.5 convolution_bitcast_fusion.1
  325.6 0.2 copy.35
  325.8 0.8 broadcast_in_dim_reshape.3
  326.6 2.0 copy.36
  328.6 2.3 gather_fusion
  330.9 0.1 copy.37
  331.0 47.2 %all-gather = f32[16,8,256]{2,1,0:T(8,128)S(1)} all-gather(f32[1,8,256]{2,1,0:T(8,128)S(1)} %copy.37), channel_id=2, replica_groups=mesh['fsdp'=64,'dp'=16] {'dp'}, dimensions={0}, use_global_device_ids=true | all-gather | bytes 139264 | tf_op jit(solution)/shard_map/all_gather | solution.py:83
  378.2 0.1 copy.38
  378.3 1.6 broadcast.96
  379.9 26.0 %scatter_fusion = f32[64,8,64]{1,2,0:T(8,128)} fusion(f32[64,8,64]{1,2,0:T(8,128)} %broadcast.96, s32[256]{0:T(256)S(1)} %bitcast.65, f32[256,8]{1,0:T(8,128)S(1)} %copy.38), kind=kCustom, calls=%fused_computation.1 | custom fusion | bytes 26624 | tf_op jit(solution)/shard_map/scatter | solution.py:60
  405.9 2.7 copy.39
  408.6 1.0 fusion.9
  409.6 0.5 convolution_bitcast_fusion
  410.1 0.2 copy.41
  410.3 0.8 reshape.75
  (6 shorter events, 0.1 us)
Async XLA Ops:
  7.2 1.6 copy-start
  7.2 314.9 %reduce-scatter.2.cloned.1.call-start = ((), (), s32[]{:S(2)}) async-start(), calls=%async_computation.1 | async-start | bytes 8519680 | tf_op jit(solution)/shard_map/reduce_scatter | solution.py:71
  14.2 0.7 copy-start.2
  14.2 307.9 %copy-start.1 = (f32[1,64,512]{2,1,0:T(8,128)S(1)}, f32[1,64,512]{2,1,0:T(8,128)}, u32[]{:S(2)}) copy-start(f32[1,64,512]{2,1,0:T(8,128)} %param.6) | copy-start | bytes 393220
Sparse Core Ops, SparseCore 0:
  14.4 307.6 reduce-scatter.1
where the time goes:
time: 424 us; the launch traced here: 418 us
  waiting for transfers between devices  306 us (72%)
  blocking collectives  47.2 us (11%)
  local copies, waits for them, and re-layouts  39 us (9%)
  between operations  14.1 us (3%)
  matrix products  9.45 us (2%)
    reduce_scatter x1, waiting for transfers between devices, shards(): lax.psum_scatter(lax.dot_general(tokens_in, grads_in, (((0,), (0,)), ((),...  306 us
    all_gather x1, blocking collectives, shards(): everyone = lax.all_gather(picked[None], 'dp', axis=0, tiled=True)  47.2 us
    scatter x2, local copies, waits for them, and re-layouts, scatter_back(): blocks.at[:, wave_row, :, wave_col].set(jnp.moveaxis(values, -1, 0))  28.7 us
  transfers between devices with their start and end apart: 1, of which 1 were waited for; matrix products, arithmetic and copies ran while one was open for 0% of the time, Pallas kernels for 0%

commit v1 on v0

v1 whole, which is shorter than its diff:
```python
import jax
import jax.numpy as jnp
import ml_dtypes
import numpy as np
from jax import lax
from jax.experimental import pallas as pl
from jax.experimental.pallas import tpu as pltpu
from jax.sharding import PartitionSpec as P

BLOCK = 64
KEEP = 256
NX = 8
NY = 4
NDP = 16
TOK = 256
COLS = 512
ROWS_A = 40
ROWS_B = BLOCK - ROWS_A
HALF_B = 16
MOMENTUM_DECAY = 0.999
BF16 = jnp.bfloat16
F32 = jnp.float32


def basis_tables():
    wave = np.arange(BLOCK)[:, None]
    sample = np.arange(BLOCK)[None, :]
    phase = ((2 * sample + 1) * wave) % (4 * BLOCK)
    scale = np.where(wave == 0, np.sqrt(1.0 / BLOCK), np.sqrt(2.0 / BLOCK))
    basis = scale * np.cos(np.pi * phase / (2.0 * BLOCK))
    high = basis.astype(ml_dtypes.bfloat16)
    low = (basis - high.astype(np.float64)).astype(ml_dtypes.bfloat16)
    return np.concatenate([high, low, high, low, high, high, low, low], axis=1)


def dot(lhs, rhs, left=1, right=0):
    return lax.dot_general(lhs, rhs, (((left,), (right,)), ((), ())), preferred_element_type=F32)


def split(values):
    high = values.astype(BF16)
    return high, (values - high.astype(F32)).astype(BF16)


def slot_of(step, way):
    if step == 1:
        return 0
    if step == 5:
        return 7
    return 2 * (step - 1) - 1 + way


def kernel(
    act, cot, mom, freq, table, newm, upd,
    act_v, cot_v, mom_v, cot_send, cot_recv, cot_peer,
    pick_send, pick_recv, kept, ga, gb, rax, ray, rby, rbx,
    rmix, rinv, ltile, pall,
    load_sem, cot_load_sem, mom_sem,
    core_send, core_recv, cot_sem,
    axs, axr, ays, ayr, bys, byr, bxs, bxr, dps, dpr,
):
    me = lax.axis_index("fsdp")
    dp = lax.axis_index("dp")
    x = me // (2 * NY)
    y = (me // 2) % NY
    core = me % 2
    base = me - 2 * NY * x
    peer = me + 1 - 2 * core
    around = (lax.rem(x + 1, NX) * (2 * NY) + base, lax.rem(x + NX - 1, NX) * (2 * NY) + base)
    inner_right = y < NY - 1
    inner_left = y > 0
    along = (jnp.where(inner_right, me + 2, me - 2), jnp.where(inner_left, me - 2, me + 2))

    def slot_x(i):
        far = 4 - (i + 1) // 2
        return lax.rem(x + jnp.where(i % 2 == 1, far, NX - far), NX)

    def load(i):
        start = pl.multiple_of(slot_x(i) * COLS, COLS)
        return pltpu.make_async_copy(act.at[0, :, pl.ds(start, COLS)], act_v.at[i], load_sem.at[i])

    cot_load = pltpu.make_async_copy(cot.at[0], cot_v, cot_load_sem)
    mom_load = pltpu.make_async_copy(mom.at[0], mom_v, mom_sem)
    cot_load.start()
    for i in range(NX):
        load(jnp.int32(i)).start()
    mom_load.start()

    barrier = pltpu.get_barrier_semaphore()

    def hello(where):
        pl.semaphore_signal(barrier, inc=1, device_id=where, device_id_type=pl.DeviceIdType.MESH)

    hello({"fsdp": peer})
    hello({"fsdp": around[0]})
    hello({"fsdp": around[1]})

    @pl.when(inner_right)
    def _():
        hello({"fsdp": along[0]})

    @pl.when(inner_left)
    def _():
        hello({"fsdp": along[1]})

    def hello_group(j, carry):
        hello({"dp": lax.rem(dp + j, NDP)})
        return carry

    lax.fori_loop(1, NDP, hello_group, 0)

    out_row = lax.broadcasted_iota(jnp.int32, (TOK, COLS), 0)
    in_col = lax.broadcasted_iota(jnp.int32, (TOK, COLS), 1)
    wanted = (out_row // BLOCK) * (2 * BLOCK) + out_row % BLOCK
    take_kept = jnp.where(in_col == wanted + core * BLOCK, 1.0, 0.0).astype(BF16)
    take_sent = jnp.where(in_col == wanted + (1 - core) * BLOCK, 1.0, 0.0).astype(BF16)

    cot_load.wait()
    cot_send[...] = cot_v[...].astype(F32)
    pl.semaphore_wait(
        barrier, 3 + (NDP - 1) + inner_right.astype(jnp.int32) + inner_left.astype(jnp.int32)
    )

    def send(src, dst, send_sem, recv_sem, where):
        return pltpu.make_async_remote_copy(
            src_ref=src, dst_ref=dst, send_sem=send_sem, recv_sem=recv_sem,
            device_id=where, device_id_type=pl.DeviceIdType.MESH,
        )

    cot_copy = send(cot_send, cot_recv, cot_sem.at[0], cot_sem.at[1], {"fsdp": peer})
    cot_copy.start()

    def swap(i):
        return send(pick_send.at[i], pick_recv.at[i], core_send.at[i], core_recv.at[i], {"fsdp": peer})

    def exchange(i, carry):
        load(i).wait()
        block = act_v[i]
        pick_send[i] = dot(take_sent, block, 1, 1)
        swap(i).start()
        kept[i] = dot(take_kept, block, 1, 1).astype(BF16)
        return carry

    lax.fori_loop(0, NX, exchange, 0)

    def ax_copy(way, step, sub):
        return send(
            ga.at[slot_of(step, way), sub], rax.at[way, step - 1, sub],
            axs.at[way, step - 1, sub], axr.at[way, step - 1, sub], {"fsdp": around[way]},
        )

    def ay_copy(way, owner):
        return send(
            ga.at[7, owner], ray.at[way, owner], ays.at[owner], ayr.at[way, owner],
            {"fsdp": along[way]},
        )

    def by_copy(way, i, owner):
        return send(
            gb.at[i, owner], rby.at[way, i, owner], bys.at[i, owner], byr.at[way, i, owner],
            {"fsdp": along[way]},
        )

    def bx_copy(way, step):
        slot = slot_of(step, way)
        if step == 1:
            rows = pl.ds(0, HALF_B) if way == 0 else pl.ds(HALF_B, ROWS_B - HALF_B)
        else:
            rows = pl.ds(0, ROWS_B)
        return send(
            gb.at[slot, y, rows], rbx.at[way, step - 1, rows],
            bxs.at[way, step - 1], bxr.at[way, step - 1], {"fsdp": around[way]},
        )

    def first_half(way, sub):
        return (sub < 2) == (way == 0)

    cot_copy.wait_recv()
    cot_peer[...] = cot_recv[...].astype(BF16)

    def product(i, carry):
        total = dot(kept[i], cot_v[...])
        swap(i).wait_recv()
        total = total + dot(pick_recv[i].astype(BF16), cot_peer[...])
        blocks = total.reshape(NY, BLOCK, COLS)
        ga[i] = blocks[:, :ROWS_A]
        gb[i] = blocks[:, ROWS_A:]

        @pl.when(i == 0)
        def _():
            for sub in range(2):
                ax_copy(0, 1, sub).start()
                ax_copy(1, 1, sub + 2).start()

        @pl.when(i == 1)
        def _():
            for sub in (2, 3):
                ax_copy(0, 2, sub).start()

        @pl.when(i == 2)
        def _():
            for sub in (0, 1):
                ax_copy(1, 2, sub).start()

        @pl.when(y == 0)
        def _():
            for owner in (3, 2, 1):
                by_copy(0, i, owner).start()

        @pl.when(y == NY - 1)
        def _():
            for owner in (0, 1, 2):
                by_copy(1, i, owner).start()

        return carry

    lax.fori_loop(0, NX, product, 0)

    wave = lax.broadcasted_iota(jnp.int32, (BLOCK, KEEP), 0)
    chosen = freq[...]
    hot_row = jnp.where(wave == chosen // BLOCK, 1.0, 0.0).astype(BF16)
    hot_col = jnp.where(wave == chosen % BLOCK, 1.0, 0.0).astype(BF16)
    rmix[...] = dot(hot_row, table[:, :256], 0, 0).astype(BF16)
    rinv[...] = dot(table[:, :128], hot_row, 0, 0).astype(BF16)
    pair = dot(hot_col, table[:, 256:], 0, 0)
    narrow = pair[:, :128] + pair[:, 128:]
    ltile[...] = jnp.concatenate([narrow] * 4, axis=1)

    def ax_round(step, sub):
        for way in (0, 1):
            if step == 2 and not first_half(way, sub):
                continue
            ax_copy(way, step - 1, sub).wait_recv()
            slot = slot_of(step, way)
            ga[slot, sub] = ga[slot, sub] + rax[way, step - 2, sub]
            if step <= 4:
                ax_copy(way, step, sub).start()

    def chain_y(total, arrived, copy):
        for k in range(NY - 2):
            right, left = NY - 1 - k, k

            @pl.when(inner_left & (y < right))
            def _(owner=right):
                copy(0, owner).wait_recv()
                total(owner)[...] = total(owner)[...] + arrived(0, owner)[...]
                copy(0, owner).start()

            @pl.when(inner_right & (y > left))
            def _(owner=left):
                copy(1, owner).wait_recv()
                total(owner)[...] = total(owner)[...] + arrived(1, owner)[...]
                copy(1, owner).start()

        @pl.when(inner_left)
        def _():
            copy(0, y).wait_recv()
            total(y)[...] = total(y)[...] + arrived(0, y)[...]

        @pl.when(inner_right)
        def _():
            copy(1, y).wait_recv()
            total(y)[...] = total(y)[...] + arrived(1, y)[...]

    def bx_round(i):
        if i == 0:
            bx_copy(0, 1).start()
            bx_copy(1, 1).start()
            return
        ways = (0, 1) if i == 7 else ((i + 1) % 2,)
        step = (i + 1) // 2 + 1
        for way in ways:
            bx_copy(way, step - 1).wait_recv()
            if step == 2:
                rows = pl.ds(0, HALF_B) if way == 0 else pl.ds(HALF_B, ROWS_B - HALF_B)
            else:
                rows = pl.ds(0, ROWS_B)
            gb[i, y, rows] = gb[i, y, rows] + rbx[way, step - 2, rows]
            if step <= 4:
                bx_copy(way, step).start()

    rounds = [(2, (0, 2)), (2, (1, 3))] + [(s, (q,)) for s in (3, 4, 5) for q in range(NY)]
    counts = [2, 2, 2, 2, 2, 2, 1, 1]
    at = 0
    for i in range(NX):
        chain_y(
            lambda o, i=i: gb.at[i, o], lambda w, o, i=i: rby.at[w, i, o],
            lambda w, o, i=i: by_copy(w, i, o),
        )
        for step, subs in rounds[at:at + counts[i]]:
            for sub in subs:
                ax_round(step, sub)
        at += counts[i]
        if i > 0:
            bx_round(i - 1)

    @pl.when(y == 0)
    def _():
        for owner in (3, 2, 1):
            ay_copy(0, owner).start()

    @pl.when(y == NY - 1)
    def _():
        for owner in (0, 1, 2):
            ay_copy(1, owner).start()

    chain_y(lambda o: ga.at[7, o], lambda w, o: ray.at[w, o], ay_copy)
    bx_round(7)

    mom_load.wait()
    gradient = jnp.concatenate([ga[7, y], gb[7, y]], axis=0)
    fresh = MOMENTUM_DECAY * mom_v[...] + gradient
    high, low = split(fresh)
    spread = dot(rmix[...], jnp.concatenate([high, high, low, low], axis=0)) * ltile[...]
    high, low = split(spread)
    block_row = lax.broadcasted_iota(jnp.int32, (8, COLS), 0)
    block_col = lax.broadcasted_iota(jnp.int32, (8, COLS), 1)
    ones = jnp.where(block_col // BLOCK == block_row, 1.0, 0.0).astype(BF16)
    picks = dot(ones, high, 1, 1) + dot(ones, low, 1, 1)
    pall[dp] = picks

    def dp_copy(to, slot):
        return send(pall.at[slot], pall.at[slot], dps.at[to], dpr.at[slot], {"dp": to})

    def share(j, carry):
        dp_copy(lax.rem(dp + j, NDP), dp).start()
        return carry

    lax.fori_loop(1, NDP, share, 0)

    def back(values):
        high, low = split(values)
        wide = dot(jnp.concatenate([high, low], axis=0), jnp.concatenate([ones, ones], axis=0), 0, 0)
        high, low = split(wide * ltile[...])
        both = dot(rinv[...], high)
        return both[:BLOCK] + both[BLOCK:] + dot(rinv[:BLOCK, :], low)

    newm[0] = fresh - back(picks)

    def gather(j, carry):
        other = lax.rem(dp + j, NDP)
        dp_copy(other, other).wait_recv()
        return carry

    lax.fori_loop(1, NDP, gather, 0)
    upd[...] = back(jnp.sum(pall[...], axis=0) * (1.0 / NDP))

    cot_copy.wait_send()

    def done_core(i, carry):
        swap(i).wait_send()
        return carry

    lax.fori_loop(0, NX, done_core, 0)
    for way in (0, 1):
        for step in range(1, 5):
            for sub in range(NY):
                if step > 1 or first_half(way, sub):
                    ax_copy(way, step, sub).wait_send()
            bx_copy(way, step).wait_send()
    for owner in range(NY):

        @pl.when(y != owner)
        def _(owner=owner):
            ay_copy(0, owner).wait_send()

            def done_y(i, carry):
                by_copy(0, i, owner).wait_send()
                return carry

            lax.fori_loop(0, NX, done_y, 0)

    def done_dp(j, carry):
        dp_copy(lax.rem(dp + j, NDP), dp).wait_send()
        return carry

    lax.fori_loop(1, NDP, done_dp, 0)


def shards(activations, cotangents, momentum, freq_index):
    vmem = pl.BlockSpec(memory_space=pltpu.VMEM)
    hbm = pl.BlockSpec(memory_space=pl.ANY)
    dma = pltpu.SemaphoreType.DMA
    return pl.pallas_call(
        kernel,
        out_shape=(
            jax.ShapeDtypeStruct((1, BLOCK, COLS), F32),
            jax.ShapeDtypeStruct((BLOCK, COLS), F32),
        ),
        in_specs=[hbm, hbm, hbm, vmem, vmem],
        out_specs=(vmem, vmem),
        scratch_shapes=[
            pltpu.VMEM((NX, TOK, COLS), BF16),
            pltpu.VMEM((TOK, COLS), BF16),
            pltpu.VMEM((BLOCK, COLS), F32),
            pltpu.VMEM((TOK, COLS), F32),
            pltpu.VMEM((TOK, COLS), F32),
            pltpu.VMEM((TOK, COLS), BF16),
            pltpu.VMEM((NX, NY * BLOCK, TOK), F32),
            pltpu.VMEM((NX, NY * BLOCK, TOK), F32),
            pltpu.VMEM((NX, NY * BLOCK, TOK), BF16),
            pltpu.VMEM((NX, NY, ROWS_A, COLS), F32),
            pltpu.VMEM((NX, NY, ROWS_B, COLS), F32),
            pltpu.VMEM((2, 4, NY, ROWS_A, COLS), F32),
            pltpu.VMEM((2, NY, ROWS_A, COLS), F32),
            pltpu.VMEM((2, NX, NY, ROWS_B, COLS), F32),
            pltpu.VMEM((2, 4, ROWS_B, COLS), F32),
            pltpu.VMEM((KEEP, 256), BF16),
            pltpu.VMEM((128, KEEP), BF16),
            pltpu.VMEM((KEEP, COLS), F32),
            pltpu.VMEM((NDP, 8, KEEP), F32),
            dma((NX,)), dma, dma,
            dma((NX,)), dma((NX,)), dma((2,)),
            dma((2, 4, NY)), dma((2, 4, NY)),
            dma((NY,)), dma((2, NY)),
            dma((NX, NY)), dma((2, NX, NY)),
            dma((2, 4)), dma((2, 4)),
            dma((NDP,)), dma((NDP,)),
        ],
        compiler_params=pltpu.CompilerParams(
            collective_id=0, has_side_effects=True, vmem_limit_bytes=48 * 1024 * 1024
        ),
    )(activations, cotangents, momentum, freq_index.reshape(1, KEEP), jnp.asarray(basis_tables()))


def solution(mesh):
    return jax.shard_map(
        shards,
        mesh=mesh,
        in_specs=(P("dp", "fsdp", None), P("dp", "fsdp", None), P("dp", "fsdp", None), P()),
        out_specs=(P("dp", "fsdp", None), P("fsdp", None)),
        check_vma=False,
    )
```

time: 424 us -> 120 us (0.28)
  the two profiles are of different devices: /device:TPU:1 before, /device:TPU:6 now
where the time goes in v1:
time: 120 us
  Pallas kernels  113 us (94%)
  local copies, waits for them, and re-layouts  6.27 us (5%)
    pallas_call x1, Pallas kernels, shards(): pl.pallas_call(kernel, out_shape=(jax.ShapeDtypeStruct((1, BLOCK, COLS),...  113 us
    unnamed x12, local copies, waits for them, and re-layouts  6.27 us

profile of v1, /device:TPU:6, one launch (start us, length us, event | category | flops | bytes accessed | tf_op | source)
XLA Modules:
  0.0 119.6 jit_solution(1842931679557539547)
XLA Ops:
  0.6 0.0 copy-start
  0.6 1.6 %copy-done = bf16[1,256,4096]{2,1,0:T(8,128)(2,1)S(1)} copy-done((bf16[1,256,4096]{2,1,0:T(8,128)(2,1)S(1)}, bf16[1,256,4096]{2,1,0:T(8,128)(2,1)}, u32[]{:S(2)}) %copy-start) | copy-done | bytes 2097176
  2.2 0.0 copy-start.1
  2.2 0.9 copy-done.1
  3.2 0.0 copy-start.2
  3.2 0.9 copy-done.2
  4.1 0.0 copy-start.3
  4.1 0.8 copy-done.3
  4.9 0.0 copy-start.4
  4.9 0.7 copy-done.4
  5.6 112.7 %shard_map.68 = (f32[1,64,512]{2,1,0:T(8,128)S(1)}, f32[64,512]{1,0:T(8,128)S(1)}) custom-call(bf16[1,256,4096]{2,1,0:T(8,128)(2,1)S(1)} %copy-done, bf16[1,256,512]{2,1,0:T(8,128)(2,1)S(1)} %copy-done.1, f32[1,64,512]{2,1,0:T(8,128)S(1)} %copy-done.2, s32[1,256]{1,0:T(1,128)S(1)} %bitcast.1, bf16[64,512]{1,0:T(8,128)(2,1)S(1)} %copy-done.3), custom_call_target="tpu_custom_call" | custom-call | tf_op jit(solution)/shard_map/pallas_call | solution.py:384
  118.3 0.7 copy.9
  119.0 0.7 copy.10
Async XLA Ops:
  0.6 1.6 %copy-start = (bf16[1,256,4096]{2,1,0:T(8,128)(2,1)S(1)}, bf16[1,256,4096]{2,1,0:T(8,128)(2,1)}, u32[]{:S(2)}) copy-start(bf16[1,256,4096]{2,1,0:T(8,128)(2,1)} %act.1) | copy-start | bytes 6291460
  2.2 0.9 copy-start.1
  3.2 0.9 copy-start.2
  4.1 0.8 copy-start.3
  4.9 0.7 copy-start.4

commit v2 on v1

v2 whole, which is shorter than its diff:
```python
import jax
import jax.numpy as jnp
import ml_dtypes
import numpy as np
from jax import lax
from jax.experimental import pallas as pl
from jax.experimental.pallas import tpu as pltpu
from jax.sharding import PartitionSpec as P

BLOCK = 64
KEEP = 256
NX = 8
NY = 4
NDP = 16
TOK = 256
COLS = 512
ROWS_A = 48
ROWS_B = BLOCK - ROWS_A
HALF_B = 8
MOMENTUM_DECAY = 0.999
BF16 = jnp.bfloat16
F32 = jnp.float32


def basis_tables():
    wave = np.arange(BLOCK)[:, None]
    sample = np.arange(BLOCK)[None, :]
    phase = ((2 * sample + 1) * wave) % (4 * BLOCK)
    scale = np.where(wave == 0, np.sqrt(1.0 / BLOCK), np.sqrt(2.0 / BLOCK))
    basis = scale * np.cos(np.pi * phase / (2.0 * BLOCK))
    high = basis.astype(ml_dtypes.bfloat16)
    low = (basis - high.astype(np.float64)).astype(ml_dtypes.bfloat16)
    return np.concatenate([high, low, high, low, high, high, low, low], axis=1)


def dot(lhs, rhs, left=1, right=0):
    return lax.dot_general(lhs, rhs, (((left,), (right,)), ((), ())), preferred_element_type=F32)


def split(values):
    high = values.astype(BF16)
    return high, (values - high.astype(F32)).astype(BF16)


def slot_of(step, way):
    if step == 1:
        return 0
    if step == 5:
        return 7
    return 2 * (step - 1) - 1 + way


def kernel(
    act, cot, mom, freq, table, newm, upd,
    act_v, cot_v, mom_v, freq_v, table_v, take_kept, take_sent, cot_send, cot_recv, cot_peer,
    pick_send, pick_recv, kept, ga, gb, rax, ray, rby, rbx,
    rmix, rinv, ltile, pall,
    load_sem, small_sem, core_send, core_recv, cot_sem,
    axs, axr, ays, ayr, bys, byr, bxs, bxr, dps, dpr,
):
    me = lax.axis_index("fsdp")
    dp = lax.axis_index("dp")
    x = me // (2 * NY)
    y = (me // 2) % NY
    core = me % 2
    base = me - 2 * NY * x
    peer = me + 1 - 2 * core
    around = (lax.rem(x + 1, NX) * (2 * NY) + base, lax.rem(x + NX - 1, NX) * (2 * NY) + base)

    def ranked(rank):
        return lax.rem(y + 1 + rank, NY)

    def slot_x(i):
        far = 4 - (i + 1) // 2
        return lax.rem(x + jnp.where(i % 2 == 1, far, NX - far), NX)

    def load(i):
        start = pl.multiple_of(slot_x(i) * COLS, COLS)
        return pltpu.make_async_copy(act.at[0, :, pl.ds(start, COLS)], act_v.at[i], load_sem.at[i])

    cot_load = pltpu.make_async_copy(cot.at[0], cot_v, small_sem.at[0])
    mom_load = pltpu.make_async_copy(mom.at[0], mom_v, small_sem.at[1])
    freq_load = pltpu.make_async_copy(freq, freq_v, small_sem.at[2])
    table_load = pltpu.make_async_copy(table, table_v, small_sem.at[3])
    cot_load.start()
    for i in range(NX):
        load(jnp.int32(i)).start()
    freq_load.start()
    table_load.start()
    mom_load.start()

    barrier = pltpu.get_barrier_semaphore()

    def hello(where):
        pl.semaphore_signal(barrier, inc=1, device_id=where, device_id_type=pl.DeviceIdType.MESH)

    def hello_group(j, carry):
        hello({"dp": lax.rem(dp + j, NDP)})
        return carry

    lax.fori_loop(1, NDP, hello_group, 0)
    for rank in range(NY - 1):
        hello({"fsdp": me + 2 * (ranked(rank) - y)})
    hello({"fsdp": around[0]})
    hello({"fsdp": around[1]})
    hello({"fsdp": peer})

    out_row = lax.broadcasted_iota(jnp.int32, (TOK, COLS), 0)
    in_col = lax.broadcasted_iota(jnp.int32, (TOK, COLS), 1)
    wanted = (out_row // BLOCK) * (2 * BLOCK) + out_row % BLOCK
    take_kept[...] = jnp.where(in_col == wanted + core * BLOCK, 1.0, 0.0).astype(BF16)
    take_sent[...] = jnp.where(in_col == wanted + (1 - core) * BLOCK, 1.0, 0.0).astype(BF16)

    def send(src, dst, send_sem, recv_sem, where):
        return pltpu.make_async_remote_copy(
            src_ref=src, dst_ref=dst, send_sem=send_sem, recv_sem=recv_sem,
            device_id=where, device_id_type=pl.DeviceIdType.MESH,
        )

    cot_copy = send(cot_send, cot_recv, cot_sem.at[0], cot_sem.at[1], {"fsdp": peer})

    def swap(i):
        return send(pick_send.at[i], pick_recv.at[i], core_send.at[i], core_recv.at[i], {"fsdp": peer})

    def pick(i):
        load(i).wait()
        pick_send[i] = dot(take_sent[...], act_v[i], 1, 1)

    def keep(i):
        kept[i] = dot(take_kept[...], act_v[i], 1, 1).astype(BF16)

    def ax_copy(way, step, rank):
        sub = ranked(rank)
        return send(
            ga.at[slot_of(step, way), sub], rax.at[way, step - 1, rank],
            axs.at[way, step - 1, rank], axr.at[way, step - 1, rank], {"fsdp": around[way]},
        )

    def to_line(rank):
        return {"fsdp": me + 2 * (ranked(rank) - y)}

    def ay_copy(rank):
        return send(
            ga.at[NX - 1, ranked(rank)], ray.at[rank], ays.at[rank], ayr.at[rank], to_line(rank)
        )

    def by_copy(i, rank):
        return send(
            gb.at[i, ranked(rank)], rby.at[i, rank], bys.at[i, rank], byr.at[i, rank], to_line(rank)
        )

    def bx_rows(way, step):
        if step > 1:
            return pl.ds(0, ROWS_B)
        return pl.ds(0, HALF_B) if way == 0 else pl.ds(HALF_B, ROWS_B - HALF_B)

    def bx_copy(way, step):
        rows = bx_rows(way, step)
        return send(
            gb.at[slot_of(step, way), y, rows], rbx.at[way, step - 1, rows],
            bxs.at[way, step - 1], bxr.at[way, step - 1], {"fsdp": around[way]},
        )

    def first_half(way, rank):
        return (rank < 2) == (way == 0)

    def product(i):
        total = dot(kept[i], cot_v[...])
        swap(i).wait_recv()
        total = total + dot(pick_recv[i].astype(BF16), cot_peer[...])
        blocks = total.reshape(NY, BLOCK, COLS)
        ga[i] = blocks[:, :ROWS_A]
        gb[i] = blocks[:, ROWS_A:]

    def by_start(i):
        for rank in range(NY - 1):
            by_copy(i, rank).start()

    cot_load.wait()
    cot_send[...] = cot_v[...].astype(F32)
    pick(jnp.int32(0))
    pl.semaphore_wait(barrier, 3 + (NY - 1) + (NDP - 1))
    cot_copy.start()
    swap(0).start()
    keep(0)
    for i in (1, 2):
        pick(jnp.int32(i))
        swap(i).start()
        keep(i)
    cot_copy.wait_recv()
    cot_peer[...] = cot_recv[...].astype(BF16)

    product(0)
    for rank in (0, 1):
        ax_copy(0, 1, rank).start()
        ax_copy(1, 1, rank + 2).start()
    by_start(0)
    product(1)
    for rank in (2, 3):
        ax_copy(0, 2, rank).start()
    product(2)
    for rank in (0, 1):
        ax_copy(1, 2, rank).start()
    by_start(1)
    by_start(2)

    def stage(i, carry):
        pick(i)
        swap(i).start()
        keep(i)
        return carry

    lax.fori_loop(3, NX, stage, 0)

    def finish(i, carry):
        product(i)
        by_start(i)
        return carry

    lax.fori_loop(3, NX, finish, 0)

    def choose():
        freq_load.wait()
        table_load.wait()
        wave = lax.broadcasted_iota(jnp.int32, (BLOCK, KEEP), 0)
        chosen = freq_v[...]
        hot_row = jnp.where(wave == chosen // BLOCK, 1.0, 0.0).astype(BF16)
        hot_col = jnp.where(wave == chosen % BLOCK, 1.0, 0.0).astype(BF16)
        rmix[...] = dot(hot_row, table_v[:, :256], 0, 0).astype(BF16)
        rinv[...] = dot(table_v[:, :128], hot_row, 0, 0).astype(BF16)
        pair = dot(hot_col, table_v[:, 256:], 0, 0)
        narrow = pair[:, :128] + pair[:, 128:]
        ltile[...] = jnp.concatenate([narrow] * 4, axis=1)

    def ax_part(way, step, rank):
        ax_copy(way, step - 1, rank).wait_recv()
        slot, sub = slot_of(step, way), ranked(rank)
        ga[slot, sub] = ga[slot, sub] + rax[way, step - 2, rank]
        if step <= 4:
            ax_copy(way, step, rank).start()

    orders = {2: ((0, 1), (2, 3)), 3: ((2, 0, 3, 1), (0, 2, 1, 3)), 4: ((0, 2, 1, 3),) * 2, 5: ((0, 2, 1, 3),) * 2}

    def ax_round(step, place):
        for way in (0, 1):
            ax_part(way, step, orders[step][way][place])
        if step == 5 and place < 3:
            ay_copy(orders[5][0][place]).start()

    def by_round(i):
        total = gb[i, y]
        for rank in range(NY - 1):
            by_copy(i, rank).wait_recv()
            total = total + rby[i, rank]
        gb[i, y] = total

    def bx_round(i):
        if i == 0:
            bx_copy(0, 1).start()
            bx_copy(1, 1).start()
            return
        ways = (0, 1) if i == 7 else ((i + 1) % 2,)
        step = (i + 1) // 2 + 1
        for way in ways:
            bx_copy(way, step - 1).wait_recv()
            rows = bx_rows(way, step - 1)
            gb[i, y, rows] = gb[i, y, rows] + rbx[way, step - 2, rows]
            if step <= 4:
                bx_copy(way, step).start()

    ax_round(2, 0)
    by_round(0)
    bx_round(0)
    ax_round(2, 1)
    by_round(1)
    ax_round(3, 0)
    choose()
    by_round(2)
    bx_round(1)
    bx_round(2)
    ax_round(3, 1)
    ax_round(3, 2)
    by_round(3)
    ax_round(3, 3)
    by_round(4)
    bx_round(3)
    bx_round(4)
    by_round(5)
    ax_round(4, 0)
    ax_round(4, 1)
    by_round(6)
    ax_round(4, 2)
    ax_round(4, 3)
    bx_round(5)
    bx_round(6)
    by_round(7)
    for place in range(NY):
        ax_round(5, place)
    bx_round(7)

    mom_load.wait()
    for rank in (0, 2, 1):
        ay_copy(rank).wait_recv()
    gradient = jnp.concatenate([ga[NX - 1, y] + (ray[0] + ray[1] + ray[2]), gb[NX - 1, y]], axis=0)
    fresh = MOMENTUM_DECAY * mom_v[...] + gradient
    high, low = split(fresh)
    spread = dot(rmix[...], jnp.concatenate([high, high, low, low], axis=0)) * ltile[...]
    high, low = split(spread)
    block_row = lax.broadcasted_iota(jnp.int32, (8, COLS), 0)
    block_col = lax.broadcasted_iota(jnp.int32, (8, COLS), 1)
    ones = jnp.where(block_col // BLOCK == block_row, 1.0, 0.0).astype(BF16)
    picks = dot(ones, high, 1, 1) + dot(ones, low, 1, 1)
    pall[dp] = picks

    def dp_copy(to, slot):
        return send(pall.at[slot], pall.at[slot], dps.at[to], dpr.at[slot], {"dp": to})

    def other(j):
        return lax.rem(dp + NDP // 2 + j, NDP)

    def share(j, carry):
        @pl.when(j != NDP // 2)
        def _():
            dp_copy(other(j), dp).start()

        return carry

    lax.fori_loop(0, NDP, share, 0)

    def back(values):
        high, low = split(values)
        wide = dot(jnp.concatenate([high, low], axis=0), jnp.concatenate([ones, ones], axis=0), 0, 0)
        high, low = split(wide * ltile[...])
        both = dot(rinv[...], high)
        return both[:BLOCK] + both[BLOCK:] + dot(rinv[:BLOCK, :], low)

    newm[0] = fresh - back(picks)

    cot_copy.wait_send()

    def done(i, carry):
        swap(i).wait_send()
        for rank in range(NY - 1):
            by_copy(i, rank).wait_send()
        return carry

    lax.fori_loop(0, NX, done, 0)
    for way in (0, 1):
        for step in range(1, 5):
            for rank in range(NY):
                if step > 1 or first_half(way, rank):
                    ax_copy(way, step, rank).wait_send()
            bx_copy(way, step).wait_send()
    for rank in range(NY - 1):
        ay_copy(rank).wait_send()

    def gather(j, carry):
        where = lax.rem(dp + j, NDP)
        dp_copy(where, where).wait_recv()
        return carry

    lax.fori_loop(1, NDP, gather, 0)
    upd[...] = back(jnp.sum(pall[...], axis=0) * (1.0 / NDP))

    def done_dp(j, carry):
        dp_copy(lax.rem(dp + j, NDP), dp).wait_send()
        return carry

    lax.fori_loop(1, NDP, done_dp, 0)


def shards(activations, cotangents, momentum, freq_index):
    vmem = pl.BlockSpec(memory_space=pltpu.VMEM)
    hbm = pl.BlockSpec(memory_space=pl.ANY)
    dma = pltpu.SemaphoreType.DMA
    return pl.pallas_call(
        kernel,
        out_shape=(
            jax.ShapeDtypeStruct((1, BLOCK, COLS), F32),
            jax.ShapeDtypeStruct((BLOCK, COLS), F32),
        ),
        in_specs=[hbm] * 5,
        out_specs=(vmem, vmem),
        scratch_shapes=[
            pltpu.VMEM((NX, TOK, COLS), BF16),
            pltpu.VMEM((TOK, COLS), BF16),
            pltpu.VMEM((BLOCK, COLS), F32),
            pltpu.VMEM((1, KEEP), jnp.int32),
            pltpu.VMEM((BLOCK, COLS), BF16),
            pltpu.VMEM((TOK, COLS), BF16),
            pltpu.VMEM((TOK, COLS), BF16),
            pltpu.VMEM((TOK, COLS), F32),
            pltpu.VMEM((TOK, COLS), F32),
            pltpu.VMEM((TOK, COLS), BF16),
            pltpu.VMEM((NX, NY * BLOCK, TOK), F32),
            pltpu.VMEM((NX, NY * BLOCK, TOK), F32),
            pltpu.VMEM((NX, NY * BLOCK, TOK), BF16),
            pltpu.VMEM((NX, NY, ROWS_A, COLS), F32),
            pltpu.VMEM((NX, NY, ROWS_B, COLS), F32),
            pltpu.VMEM((2, 4, NY, ROWS_A, COLS), F32),
            pltpu.VMEM((NY - 1, ROWS_A, COLS), F32),
            pltpu.VMEM((NX, NY - 1, ROWS_B, COLS), F32),
            pltpu.VMEM((2, 4, ROWS_B, COLS), F32),
            pltpu.VMEM((KEEP, 256), BF16),
            pltpu.VMEM((128, KEEP), BF16),
            pltpu.VMEM((KEEP, COLS), F32),
            pltpu.VMEM((NDP, 8, KEEP), F32),
            dma((NX,)), dma((4,)), dma((NX,)), dma((NX,)), dma((2,)),
            dma((2, 4, NY)), dma((2, 4, NY)),
            dma((NY - 1,)), dma((NY - 1,)),
            dma((NX, NY - 1)), dma((NX, NY - 1)),
            dma((2, 4)), dma((2, 4)),
            dma((NDP,)), dma((NDP,)),
        ],
        compiler_params=pltpu.CompilerParams(
            collective_id=0, has_side_effects=True, vmem_limit_bytes=62 * 1024 * 1024
        ),
    )(activations, cotangents, momentum, freq_index.reshape(1, KEEP), jnp.asarray(basis_tables()))


def solution(mesh):
    return jax.shard_map(
        shards,
        mesh=mesh,
        in_specs=(P("dp", "fsdp", None), P("dp", "fsdp", None), P("dp", "fsdp", None), P()),
        out_specs=(P("dp", "fsdp", None), P("fsdp", None)),
        check_vma=False,
    )
```

time: 120 us -> 80.5 us (0.67)
  the two profiles are of different devices: /device:TPU:6 before, /device:TPU:1 now
where the time goes in v2:
time: 80.5 us; the launch traced here: 80.3 us
  Pallas kernels  76.6 us (95%)
  local copies, waits for them, and re-layouts  3.14 us (4%)
    pallas_call x1, Pallas kernels, shards(): pl.pallas_call(kernel, out_shape=(jax.ShapeDtypeStruct((1, BLOCK, COLS),...  76.6 us
    unnamed x2, local copies, waits for them, and re-layouts  3.14 us

profile of v2, /device:TPU:1, one launch (start us, length us, event | category | flops | bytes accessed | tf_op | source)
XLA Modules:
  0.0 80.3 jit_solution(659786425986950833)
XLA Ops:
  0.6 76.6 %shard_map.68 = (f32[1,64,512]{2,1,0:T(8,128)}, f32[64,512]{1,0:T(8,128)}) custom-call(bf16[1,256,4096]{2,1,0:T(8,128)(2,1)} %act.1, bf16[1,256,512]{2,1,0:T(8,128)(2,1)} %cot.1, f32[1,64,512]{2,1,0:T(8,128)} %mom.1, s32[1,256]{1,0:T(1,128)} %bitcast.1, bf16[64,512]{1,0:T(8,128)(2,1)} %constant.2.clone.table), custom_call_target="tpu_custom_call" | custom-call | tf_op jit(solution)/shard_map/pallas_call | solution.py:376
  77.2 1.6 %copy.9 = f32[1,64,512]{2,1,0:T(8,128)} copy(f32[1,64,512]{2,1,0:T(8,128)} %get-tuple-element.4) | data formatting | bytes 262144
  78.8 1.6 %copy.10 = f32[64,512]{1,0:T(8,128)} copy(f32[64,512]{1,0:T(8,128)} %get-tuple-element.5) | data formatting | bytes 262144

commit v3 on v2

--- a/solution.py
+++ b/solution.py
@@ -54,9 +54,9 @@
     act, cot, mom, freq, table, newm, upd,
     act_v, cot_v, mom_v, freq_v, table_v, take_kept, take_sent, cot_send, cot_recv, cot_peer,
     pick_send, pick_recv, kept, ga, gb, rax, ray, rby, rbx,
-    rmix, rinv, ltile, pall,
-    load_sem, small_sem, core_send, core_recv, cot_sem,
-    axs, axr, ays, ayr, bys, byr, bxs, bxr, dps, dpr,
+    rmix, rinv, ltile, held, pg, psum, rpy, rpx, pall,
+    gate, load_sem, small_sem, core_send, core_recv, cot_sem,
+    axs, axr, ays, ayr, bys, byr, bxs, bxr, pys, pyr, pxs, pxr, dps, dpr,
 ):
     me = lax.axis_index("fsdp")
     dp = lax.axis_index("dp")
@@ -95,15 +95,22 @@
         pl.semaphore_signal(barrier, inc=1, device_id=where, device_id_type=pl.DeviceIdType.MESH)
 
     def hello_group(j, carry):
-        hello({"dp": lax.rem(dp + j, NDP)})
-        return carry
+        hello({"fsdp": me - core + 1, "dp": lax.rem(dp + j, NDP)})
+        return carry
+
+    def hello_ring(j, carry):
+        hello({"fsdp": lax.rem(x + j, NX) * (2 * NY) + 2 * y})
+        return carry
+
+    lax.fori_loop(1, NX, hello_ring, 0)
+    for rank in range(NY - 1):
+        hello({"fsdp": 2 * (NY * x + ranked(rank))})
+
+    @pl.when(core == 1)
+    def _():
+        hello({"fsdp": peer})
 
     lax.fori_loop(1, NDP, hello_group, 0)
-    for rank in range(NY - 1):
-        hello({"fsdp": me + 2 * (ranked(rank) - y)})
-    hello({"fsdp": around[0]})
-    hello({"fsdp": around[1]})
-    hello({"fsdp": peer})
 
     out_row = lax.broadcasted_iota(jnp.int32, (TOK, COLS), 0)
     in_col = lax.broadcasted_iota(jnp.int32, (TOK, COLS), 1)
@@ -129,10 +136,14 @@
     def keep(i):
         kept[i] = dot(take_kept[...], act_v[i], 1, 1).astype(BF16)
 
+    def first_half(way, rank):
+        return (rank < 2) == (way == 0)
+
     def ax_copy(way, step, rank):
-        sub = ranked(rank)
+        raw = step == 1 or (step == 2 and not first_half(way, rank))
         return send(
-            ga.at[slot_of(step, way), sub], rax.at[way, step - 1, rank],
+            ga.at[slot_of(step, way), ranked(rank)] if raw else rax.at[way, step - 2, rank],
+            rax.at[way, step - 1, rank],
             axs.at[way, step - 1, rank], axr.at[way, step - 1, rank], {"fsdp": around[way]},
         )
 
@@ -148,6 +159,20 @@
         return send(
             gb.at[i, ranked(rank)], rby.at[i, rank], bys.at[i, rank], byr.at[i, rank], to_line(rank)
         )
+
+    def py_copy(i, rank):
+        return send(
+            pg.at[i, ranked(rank)], rpy.at[i, rank], pys.at[i, rank], pyr.at[i, rank], to_line(rank)
+        )
+
+    def px_copy(i):
+        return send(
+            psum.at[i], rpx.at[i], pxs.at[i], pxr.at[i],
+            {"fsdp": slot_x(i) * (2 * NY) + base},
+        )
+
+    def dp_copy(to, slot):
+        return send(pall.at[slot], pall.at[slot], dps.at[to], dpr.at[slot], {"dp": to})
 
     def bx_rows(way, step):
         if step > 1:
@@ -157,12 +182,9 @@
     def bx_copy(way, step):
         rows = bx_rows(way, step)
         return send(
-            gb.at[slot_of(step, way), y, rows], rbx.at[way, step - 1, rows],
+            rby.at[slot_of(step, way), 0, rows], rbx.at[way, step - 1, rows],
             bxs.at[way, step - 1], bxr.at[way, step - 1], {"fsdp": around[way]},
         )
-
-    def first_half(way, rank):
-        return (rank < 2) == (way == 0)
 
     def product(i):
         total = dot(kept[i], cot_v[...])
@@ -179,7 +201,18 @@
     cot_load.wait()
     cot_send[...] = cot_v[...].astype(F32)
     pick(jnp.int32(0))
-    pl.semaphore_wait(barrier, 3 + (NY - 1) + (NDP - 1))
+
+    @pl.when(core == 0)
+    def _():
+        pl.semaphore_wait(barrier, 2 * (NX - 1) + 2 * (NY - 1) + 1)
+        pl.semaphore_signal(
+            gate.at[0], inc=1, device_id={"fsdp": peer}, device_id_type=pl.DeviceIdType.MESH
+        )
+
+    @pl.when(core == 1)
+    def _():
+        pl.semaphore_wait(gate.at[0], 1)
+
     cot_copy.start()
     swap(0).start()
     keep(0)
@@ -214,7 +247,6 @@
 
     def finish(i, carry):
         product(i)
-        by_start(i)
         return carry
 
     lax.fori_loop(3, NX, finish, 0)
@@ -235,24 +267,28 @@
     def ax_part(way, step, rank):
         ax_copy(way, step - 1, rank).wait_recv()
         slot, sub = slot_of(step, way), ranked(rank)
-        ga[slot, sub] = ga[slot, sub] + rax[way, step - 2, rank]
+        rax[way, step - 2, rank] = ga[slot, sub] + rax[way, step - 2, rank]
+        ax_copy(way, step, rank).start()
+
+    orders = {2: ((0, 1), (2, 3)), 3: ((2, 0, 3, 1), (0, 2, 1, 3)), 4: ((0, 2, 1, 3),) * 2, 5: ((0, 2, 1, 3),) * 2}
+
+    def ax_round(step, place):
         if step <= 4:
-            ax_copy(way, step, rank).start()
-
-    orders = {2: ((0, 1), (2, 3)), 3: ((2, 0, 3, 1), (0, 2, 1, 3)), 4: ((0, 2, 1, 3),) * 2, 5: ((0, 2, 1, 3),) * 2}
-
-    def ax_round(step, place):
+            for way in (0, 1):
+                ax_part(way, step, orders[step][way][place])
+            return
+        rank = orders[5][0][place]
         for way in (0, 1):
-            ax_part(way, step, orders[step][way][place])
-        if step == 5 and place < 3:
-            ay_copy(orders[5][0][place]).start()
+            ax_copy(way, 4, rank).wait_recv()
+        sub = ranked(rank)
+        ga[NX - 1, sub] = ga[NX - 1, sub] + (rax[0, 3, rank] + rax[1, 3, rank])
+        if rank < 3:
+            ay_copy(rank).start()
 
     def by_round(i):
-        total = gb[i, y]
         for rank in range(NY - 1):
             by_copy(i, rank).wait_recv()
-            total = total + rby[i, rank]
-        gb[i, y] = total
+        rby[i, 0] = gb[i, y] + rby[i, 0] + rby[i, 1] + rby[i, 2]
 
     def bx_round(i):
         if i == 0:
@@ -264,77 +300,130 @@
         for way in ways:
             bx_copy(way, step - 1).wait_recv()
             rows = bx_rows(way, step - 1)
-            gb[i, y, rows] = gb[i, y, rows] + rbx[way, step - 2, rows]
+            rby[i, 0, rows] = rby[i, 0, rows] + rbx[way, step - 2, rows]
             if step <= 4:
                 bx_copy(way, step).start()
 
+    block_row = lax.broadcasted_iota(jnp.int32, (8, COLS), 0)
+    block_col = lax.broadcasted_iota(jnp.int32, (8, COLS), 1)
+    ones = jnp.where(block_col // BLOCK == block_row, 1.0, 0.0).astype(BF16)
+
+    def picks_of(rows):
+        high, low = split(rows)
+        spread = dot(rmix[...], jnp.concatenate([high, high, low, low], axis=0)) * ltile[...]
+        high, low = split(spread)
+        return dot(ones, high, 1, 1) + dot(ones, low, 1, 1)
+
+    def back(values):
+        high, low = split(values)
+        wide = dot(jnp.concatenate([high, low], axis=0), jnp.concatenate([ones, ones], axis=0), 0, 0)
+        high, low = split(wide * ltile[...])
+        both = dot(rinv[...], high)
+        return both[:BLOCK] + both[BLOCK:] + dot(rinv[:BLOCK, :], low)
+
+    def partial(i, carry):
+        for sub in range(NY):
+            pg[i, sub] = picks_of(jnp.concatenate([ga[i, sub], gb[i, sub]], axis=0))
+        for rank in range(NY - 1):
+            py_copy(i, rank).start()
+        return carry
+
+    def partials(first):
+        lax.fori_loop(first, first + 2, partial, 0)
+
+    def line_sum(i, carry):
+        for rank in range(NY - 1):
+            py_copy(i, rank).wait_recv()
+        psum[i] = pg[i, y] + rpy[i, 0] + rpy[i, 1] + rpy[i, 2]
+
+        @pl.when(i < NX - 1)
+        def _():
+            px_copy(i).start()
+
+        return carry
+
+    def group_sum():
+        total = psum[NX - 1] + picks_of(held[...])
+        for i in range(NX - 1):
+            px_copy(i).wait_recv()
+            total = total + rpx[i]
+        pall[dp] = total
+
+        @pl.when(core == 1)
+        def _():
+            pl.semaphore_wait(barrier, 2 * (NDP - 1))
+            pl.semaphore_signal(
+                gate.at[1], inc=1, device_id={"fsdp": peer}, device_id_type=pl.DeviceIdType.MESH
+            )
+
+        @pl.when(core == 0)
+        def _():
+            pl.semaphore_wait(gate.at[1], 1)
+
+        def share(j, carry):
+            @pl.when(j != NDP // 2)
+            def _():
+                dp_copy(lax.rem(dp + NDP // 2 + j, NDP), dp).start()
+
+            return carry
+
+        lax.fori_loop(0, NDP, share, 0)
+        held[...] = held[...] - back(total)
+
+    choose()
+    by_start(3)
     ax_round(2, 0)
+    ax_round(2, 1)
+    partials(0)
+    by_start(4)
+    ax_round(3, 0)
+    partials(2)
+    by_start(5)
     by_round(0)
     bx_round(0)
-    ax_round(2, 1)
+    ax_round(3, 1)
+    ax_round(3, 2)
+    ax_round(3, 3)
+    partials(4)
+    by_start(6)
     by_round(1)
-    ax_round(3, 0)
-    choose()
     by_round(2)
     bx_round(1)
     bx_round(2)
-    ax_round(3, 1)
-    ax_round(3, 2)
+    ax_round(4, 0)
+    partials(6)
+    by_start(7)
+    mom_load.wait()
+    held[...] = MOMENTUM_DECAY * mom_v[...]
+    ax_round(4, 1)
+    lax.fori_loop(0, NX, line_sum, 0)
     by_round(3)
-    ax_round(3, 3)
     by_round(4)
     bx_round(3)
     bx_round(4)
-    by_round(5)
-    ax_round(4, 0)
-    ax_round(4, 1)
-    by_round(6)
     ax_round(4, 2)
     ax_round(4, 3)
+    group_sum()
+    by_round(5)
+    by_round(6)
     bx_round(5)
     bx_round(6)
     by_round(7)
     for place in range(NY):
         ax_round(5, place)
     bx_round(7)
-
-    mom_load.wait()
     for rank in (0, 2, 1):
         ay_copy(rank).wait_recv()
-    gradient = jnp.concatenate([ga[NX - 1, y] + (ray[0] + ray[1] + ray[2]), gb[NX - 1, y]], axis=0)
-    fresh = MOMENTUM_DECAY * mom_v[...] + gradient
-    high, low = split(fresh)
-    spread = dot(rmix[...], jnp.concatenate([high, high, low, low], axis=0)) * ltile[...]
-    high, low = split(spread)
-    block_row = lax.broadcasted_iota(jnp.int32, (8, COLS), 0)
-    block_col = lax.broadcasted_iota(jnp.int32, (8, COLS), 1)
-    ones = jnp.where(block_col // BLOCK == block_row, 1.0, 0.0).astype(BF16)
-    picks = dot(ones, high, 1, 1) + dot(ones, low, 1, 1)
-    pall[dp] = picks
-
-    def dp_copy(to, slot):
-        return send(pall.at[slot], pall.at[slot], dps.at[to], dpr.at[slot], {"dp": to})
-
-    def other(j):
-        return lax.rem(dp + NDP // 2 + j, NDP)
-
-    def share(j, carry):
-        @pl.when(j != NDP // 2)
-        def _():
-            dp_copy(other(j), dp).start()
-
-        return carry
-
-    lax.fori_loop(0, NDP, share, 0)
-
-    def back(values):
-        high, low = split(values)
-        wide = dot(jnp.concatenate([high, low], axis=0), jnp.concatenate([ones, ones], axis=0), 0, 0)
-        high, low = split(wide * ltile[...])
-        both = dot(rinv[...], high)
-        return both[:BLOCK] + both[BLOCK:] + dot(rinv[:BLOCK, :], low)
-
-    newm[0] = fresh - back(picks)
+    gradient = jnp.concatenate([ga[NX - 1, y] + (ray[0] + ray[1] + ray[2]), rby[NX - 1, 0]], axis=0)
+    newm[0] = held[...] + gradient
+
+    def gather(j, carry):
+        where = lax.rem(dp + j, NDP)
+        dp_copy(where, where).wait_recv()
+        return carry
+
+    lax.fori_loop(1, NDP, gather, 0)
+    upd[...] = back(jnp.sum(pall[...], axis=0) * (1.0 / NDP))
 
     cot_copy.wait_send()
 
@@ -342,6 +431,12 @@
         swap(i).wait_send()
         for rank in range(NY - 1):
             by_copy(i, rank).wait_send()
+            py_copy(i, rank).wait_send()
+
+        @pl.when(i < NX - 1)
+        def _():
+            px_copy(i).wait_send()
+
         return carry
 
     lax.fori_loop(0, NX, done, 0)
@@ -353,14 +448,6 @@
             bx_copy(way, step).wait_send()
     for rank in range(NY - 1):
         ay_copy(rank).wait_send()
-
-    def gather(j, carry):
-        where = lax.rem(dp + j, NDP)
-        dp_copy(where, where).wait_recv()
-        return carry
-
-    lax.fori_loop(1, NDP, gather, 0)
-    upd[...] = back(jnp.sum(pall[...], axis=0) * (1.0 / NDP))
 
     def done_dp(j, carry):
         dp_copy(lax.rem(dp + j, NDP), dp).wait_send()
@@ -404,12 +491,19 @@
             pltpu.VMEM((KEEP, 256), BF16),
             pltpu.VMEM((128, KEEP), BF16),
             pltpu.VMEM((KEEP, COLS), F32),
+            pltpu.VMEM((BLOCK, COLS), F32),
+            pltpu.VMEM((NX, NY, 8, KEEP), F32),
+            pltpu.VMEM((NX, 8, KEEP), F32),
+            pltpu.VMEM((NX, NY - 1, 8, KEEP), F32),
+            pltpu.VMEM((NX - 1, 8, KEEP), F32),
             pltpu.VMEM((NDP, 8, KEEP), F32),
+            pltpu.SemaphoreType.REGULAR((2,)),
             dma((NX,)), dma((4,)), dma((NX,)), dma((NX,)), dma((2,)),
             dma((2, 4, NY)), dma((2, 4, NY)),
             dma((NY - 1,)), dma((NY - 1,)),
             dma((NX, NY - 1)), dma((NX, NY - 1)),
             dma((2, 4)), dma((2, 4)),
+            dma((NX, NY - 1)), dma((NX, NY - 1)), dma((NX - 1,)), dma((NX - 1,)),
             dma((NDP,)), dma((NDP,)),
         ],
         compiler_params=pltpu.CompilerParams(

time: 80.5 us -> 70.8 us (0.88)
  the two profiles are of different devices: /device:TPU:1 before, /device:TPU:16 now
where the time goes in v3:
time: 70.8 us; the launch traced here: 70.6 us
  Pallas kernels  66.8 us (94%)
  local copies, waits for them, and re-layouts  3.14 us (4%)
    pallas_call x1, Pallas kernels, shards(): pl.pallas_call(kernel, out_shape=(jax.ShapeDtypeStruct((1, BLOCK, COLS),...  66.8 us
    unnamed x2, local copies, waits for them, and re-layouts  3.14 us

profile of v3, /device:TPU:16, one launch (start us, length us, event | category | flops | bytes accessed | tf_op | source)
XLA Modules:
  0.0 70.6 jit_solution(6865249218004897200)
XLA Ops:
  0.6 66.8 %shard_map.68 = (f32[1,64,512]{2,1,0:T(8,128)}, f32[64,512]{1,0:T(8,128)}) custom-call(bf16[1,256,4096]{2,1,0:T(8,128)(2,1)} %act.1, bf16[1,256,512]{2,1,0:T(8,128)(2,1)} %cot.1, f32[1,64,512]{2,1,0:T(8,128)} %mom.1, s32[1,256]{1,0:T(1,128)} %bitcast.1, bf16[64,512]{1,0:T(8,128)(2,1)} %constant.2.clone.table), custom_call_target="tpu_custom_call" | custom-call | tf_op jit(solution)/shard_map/pallas_call | solution.py:463
  67.4 1.6 %copy.9 = f32[1,64,512]{2,1,0:T(8,128)} copy(f32[1,64,512]{2,1,0:T(8,128)} %get-tuple-element.4) | data formatting | bytes 262144
  69.0 1.6 %copy.10 = f32[64,512]{1,0:T(8,128)} copy(f32[64,512]{1,0:T(8,128)} %get-tuple-element.5) | data formatting | bytes 262144

commit v4 on v3

--- a/solution.py
+++ b/solution.py
@@ -371,39 +371,39 @@
         held[...] = held[...] - back(total)
 
     choose()
-    by_start(3)
     ax_round(2, 0)
     ax_round(2, 1)
     partials(0)
-    by_start(4)
     ax_round(3, 0)
     partials(2)
-    by_start(5)
+    by_start(3)
+    ax_round(3, 1)
+    partials(4)
+    by_start(4)
+    ax_round(3, 2)
+    ax_round(3, 3)
     by_round(0)
     bx_round(0)
-    ax_round(3, 1)
-    ax_round(3, 2)
-    ax_round(3, 3)
-    partials(4)
+    partials(6)
+    by_start(5)
+    mom_load.wait()
+    held[...] = MOMENTUM_DECAY * mom_v[...]
+    lax.fori_loop(0, NX, line_sum, 0)
     by_start(6)
     by_round(1)
+    bx_round(1)
     by_round(2)
-    bx_round(1)
     bx_round(2)
     ax_round(4, 0)
-    partials(6)
+    ax_round(4, 1)
     by_start(7)
-    mom_load.wait()
-    held[...] = MOMENTUM_DECAY * mom_v[...]
-    ax_round(4, 1)
-    lax.fori_loop(0, NX, line_sum, 0)
+    group_sum()
     by_round(3)
     by_round(4)
     bx_round(3)
     bx_round(4)
     ax_round(4, 2)
     ax_round(4, 3)
-    group_sum()
     by_round(5)
     by_round(6)
     bx_round(5)

time: 70.8 us -> 67.2 us (0.949)
  the two profiles are of different devices: /device:TPU:16 before, /device:TPU:1 now
where the time goes in v4:
time: 67.2 us; the launch traced here: 67 us
  Pallas kernels  63.2 us (94%)
  local copies, waits for them, and re-layouts  3.14 us (5%)
    pallas_call x1, Pallas kernels, shards(): pl.pallas_call(kernel, out_shape=(jax.ShapeDtypeStruct((1, BLOCK, COLS),...  63.2 us
    unnamed x2, local copies, waits for them, and re-layouts  3.14 us

profile of v4, /device:TPU:1, one launch (start us, length us, event | category | flops | bytes accessed | tf_op | source)
XLA Modules:
  0.0 67.0 jit_solution(3160381654079276242)
XLA Ops:
  0.6 63.2 %shard_map.68 = (f32[1,64,512]{2,1,0:T(8,128)}, f32[64,512]{1,0:T(8,128)}) custom-call(bf16[1,256,4096]{2,1,0:T(8,128)(2,1)} %act.1, bf16[1,256,512]{2,1,0:T(8,128)(2,1)} %cot.1, f32[1,64,512]{2,1,0:T(8,128)} %mom.1, s32[1,256]{1,0:T(1,128)} %bitcast.1, bf16[64,512]{1,0:T(8,128)(2,1)} %constant.2.clone.table), custom_call_target="tpu_custom_call" | custom-call | tf_op jit(solution)/shard_map/pallas_call | solution.py:463
  63.9 1.6 %copy.9 = f32[1,64,512]{2,1,0:T(8,128)} copy(f32[1,64,512]{2,1,0:T(8,128)} %get-tuple-element.4) | data formatting | bytes 262144
  65.4 1.6 %copy.10 = f32[64,512]{1,0:T(8,128)} copy(f32[64,512]{1,0:T(8,128)} %get-tuple-element.5) | data formatting | bytes 262144

commit v5 on v4

--- a/solution.py
+++ b/solution.py
@@ -51,7 +51,7 @@
 
 
 def kernel(
-    act, cot, mom, freq, table, newm, upd,
+    act, cot, mom, freq, table, both_out,
     act_v, cot_v, mom_v, freq_v, table_v, take_kept, take_sent, cot_send, cot_recv, cot_peer,
     pick_send, pick_recv, kept, ga, gb, rax, ray, rby, rbx,
     rmix, rinv, ltile, held, pg, psum, rpy, rpx, pall,
@@ -384,11 +384,12 @@
     ax_round(3, 3)
     by_round(0)
     bx_round(0)
+    lax.fori_loop(0, 4, line_sum, 0)
     partials(6)
     by_start(5)
     mom_load.wait()
     held[...] = MOMENTUM_DECAY * mom_v[...]
-    lax.fori_loop(0, NX, line_sum, 0)
+    lax.fori_loop(4, NX, line_sum, 0)
     by_start(6)
     by_round(1)
     bx_round(1)
@@ -409,13 +410,45 @@
     bx_round(5)
     bx_round(6)
     by_round(7)
+    cot_copy.wait_send()
+
+    def done(i, carry):
+        swap(i).wait_send()
+        for rank in range(NY - 1):
+            by_copy(i, rank).wait_send()
+            py_copy(i, rank).wait_send()
+
+        @pl.when(i < NX - 1)
+        def _():
+            px_copy(i).wait_send()
+
+        return carry
+
+    def done_ring(first, last):
+        for way in (0, 1):
+            for step in range(first, last + 1):
+                for rank in range(NY):
+                    if step > 1 or first_half(way, rank):
+                        ax_copy(way, step, rank).wait_send()
+                bx_copy(way, step).wait_send()
+
+    def done_dp(j, carry):
+        dp_copy(lax.rem(dp + j, NDP), dp).wait_send()
+        return carry
+
+    lax.fori_loop(0, NX, done, 0)
+    lax.fori_loop(1, NDP, done_dp, 0)
+    done_ring(1, 2)
     for place in range(NY):
         ax_round(5, place)
     bx_round(7)
     for rank in (0, 2, 1):
         ay_copy(rank).wait_recv()
     gradient = jnp.concatenate([ga[NX - 1, y] + (ray[0] + ray[1] + ray[2]), rby[NX - 1, 0]], axis=0)
-    newm[0] = held[...] + gradient
+    both_out[0] = held[...] + gradient
+    done_ring(3, 4)
+    for rank in range(NY - 1):
+        ay_copy(rank).wait_send()
 
     def gather(j, carry):
         where = lax.rem(dp + j, NDP)
@@ -423,51 +456,18 @@
         return carry
 
     lax.fori_loop(1, NDP, gather, 0)
-    upd[...] = back(jnp.sum(pall[...], axis=0) * (1.0 / NDP))
-
-    cot_copy.wait_send()
-
-    def done(i, carry):
-        swap(i).wait_send()
-        for rank in range(NY - 1):
-            by_copy(i, rank).wait_send()
-            py_copy(i, rank).wait_send()
-
-        @pl.when(i < NX - 1)
-        def _():
-            px_copy(i).wait_send()
-
-        return carry
-
-    lax.fori_loop(0, NX, done, 0)
-    for way in (0, 1):
-        for step in range(1, 5):
-            for rank in range(NY):
-                if step > 1 or first_half(way, rank):
-                    ax_copy(way, step, rank).wait_send()
-            bx_copy(way, step).wait_send()
-    for rank in range(NY - 1):
-        ay_copy(rank).wait_send()
-
-    def done_dp(j, carry):
-        dp_copy(lax.rem(dp + j, NDP), dp).wait_send()
-        return carry
-
-    lax.fori_loop(1, NDP, done_dp, 0)
+    both_out[1] = back(jnp.sum(pall[...], axis=0) * (1.0 / NDP))
 
 
 def shards(activations, cotangents, momentum, freq_index):
     vmem = pl.BlockSpec(memory_space=pltpu.VMEM)
     hbm = pl.BlockSpec(memory_space=pl.ANY)
     dma = pltpu.SemaphoreType.DMA
-    return pl.pallas_call(
+    result = pl.pallas_call(
         kernel,
-        out_shape=(
-            jax.ShapeDtypeStruct((1, BLOCK, COLS), F32),
-            jax.ShapeDtypeStruct((BLOCK, COLS), F32),
-        ),
+        out_shape=jax.ShapeDtypeStruct((2, BLOCK, COLS), F32),
         in_specs=[hbm] * 5,
-        out_specs=(vmem, vmem),
+        out_specs=vmem,
         scratch_shapes=[
             pltpu.VMEM((NX, TOK, COLS), BF16),
             pltpu.VMEM((TOK, COLS), BF16),
@@ -510,6 +510,7 @@
             collective_id=0, has_side_effects=True, vmem_limit_bytes=62 * 1024 * 1024
         ),
     )(activations, cotangents, momentum, freq_index.reshape(1, KEEP), jnp.asarray(basis_tables()))
+    return result[:1], result[1]
 
 
 def solution(mesh):

time: 67.2 us -> 65.5 us (0.975)
  local copies, waits for them, and re-layouts: 3.14 us -> 1.69 us
    unnamed x2 -> x0, local copies, waits for them, and re-layouts: 3.14 us -> none
    squeeze x0 -> x1, local copies, waits for them, and re-layouts: none -> 1.69 us  [shards(): return (result[:1], result[1])]
where the time goes in v5:
time: 65.5 us; the launch traced here: 65.2 us
  Pallas kernels  62.9 us (96%)
  local copies, waits for them, and re-layouts  1.69 us (3%)
    pallas_call x1, Pallas kernels, shards(): pl.pallas_call(kernel, out_shape=jax.ShapeDtypeStruct((2, BLOCK, COLS), F...  62.9 us
    squeeze x1, local copies, waits for them, and re-layouts, shards(): return (result[:1], result[1])  1.69 us

profile of v5, /device:TPU:1, one launch (start us, length us, event | category | flops | bytes accessed | tf_op | source)
XLA Modules:
  0.0 65.2 jit_solution(11241803786904667185)
XLA Ops:
  0.6 62.9 %shard_map.68 = f32[2,64,512]{2,1,0:T(8,128)} custom-call(bf16[1,256,4096]{2,1,0:T(8,128)(2,1)} %act.1, bf16[1,256,512]{2,1,0:T(8,128)(2,1)} %cot.1, f32[1,64,512]{2,1,0:T(8,128)} %mom.1, s32[1,256]{1,0:T(1,128)} %bitcast.3, bf16[64,512]{1,0:T(8,128)(2,1)} %constant.2.clone.table), custom_call_target="tpu_custom_call" | custom-call | tf_op jit(solution)/shard_map/pallas_call | solution.py:466
  63.5 1.7 %slice_bitcast_fusion = (f32[64,512]{1,0:T(8,128)}, f32[1,64,512]{2,1,0:T(8,128)}) fusion(f32[2,64,512]{2,1,0:T(8,128)} %shard_map.68), kind=kLoop, calls=%fused_computation | loop fusion | bytes 524288 | tf_op jit(solution)/shard_map/squeeze | solution.py:513
